TPU v7x, 256 devices: a whole 4x4x8 slice. The times are simulated.
256 devices in a mesh: grp: 8 (over y, z_lo), ep: 32 (over z_hi, x, core).
Axes of the slice: x: 4, y: 4, z: 8 (z_hi: 4, z_lo: 2; z = z_hi * 2 + z_lo), core: 2. Of those that a mesh axis runs over, the one named last changes fastest.
Arguments:
- tokens: bfloat16 [2, 16384, 3584], P(None, ('grp', 'ep')), may hold values from -6 to 6
- expert_ids: int32 [2, 16384, 2], P(None, ('grp', 'ep')), may hold values from 0 to 7, all different within a row; in each aligned block of 64 rows (0 to 63, 64 to 127, ..., all dimensions but the last counted through in order) at most 20 rows name the same one
- gate_weights: float32 [2, 16384, 2], P(None, ('grp', 'ep')), may hold values from 0.1 to 1
- donor_group: int32 [8, 32], replicated, may hold values from 0 to 7
- gate_pieces: bfloat16 [256, 3584, 256], P(('grp', 'ep')), may hold values from -0.09375 to 0.09375
- up_pieces: bfloat16 [256, 3584, 256], P(('grp', 'ep')), may hold values from -0.09375 to 0.09375
- down_pieces: bfloat16 [256, 3584, 256], P(('grp', 'ep')), may hold values from -0.1875 to 0.1875
Outputs:
- mixed: bfloat16 [2, 16384, 3584], P(None, ('grp', 'ep'))
- landed: bfloat16 [3, 114688, 256], P(None, ('grp', 'ep'))
Inputs may be any that keep to these rules, and one draw needn't show every extreme that they name: `expert_ids`: within each aligned block of 64 rows (one device's tokens of one micro-batch) no expert is named by more than 20 rows, and that bound is reached; each row names 2 different experts. `donor_group`: A group may name itself, and then the slot takes its own rows.
All inputs are finite; a program needn't handle non-finite values.
Results may differ from a plain program's by a relative error of at most 0.0058.
Values may be sent and summed in bfloat16 or wider, within the bound.
A program may use at most 128 MiB of HBM per device.

v0:
```python
import jax
import jax.numpy as jnp
from jax import lax
from jax.sharding import PartitionSpec as P

SPLIT = 4
SECTIONS = 8


def slot_table(picked_ids, experts, capacity):
    row_count, chosen = picked_ids.shape
    flat_picks = picked_ids.reshape(row_count * chosen)
    onehot = (flat_picks[:, None] == jnp.arange(experts, dtype=jnp.int32)[None, :]).astype(
        jnp.int32
    )
    earlier = jnp.cumsum(onehot, axis=0) - onehot
    slot_ranks = jnp.sum(earlier * onehot, axis=1)
    slot_index = flat_picks * capacity + slot_ranks
    anchor = jnp.arange(row_count * chosen, dtype=jnp.int32) // chosen
    sources = jnp.zeros((experts * capacity,), jnp.int32).at[slot_index].set(anchor)
    filled = jnp.zeros((experts * capacity,), jnp.int32).at[slot_index].set(1)
    return (slot_index.reshape(row_count, chosen), sources, filled)


def pack_rows(block_tokens, sources, filled, experts, capacity):
    gathered = jnp.take(block_tokens, sources, axis=0)
    kept_rows = jnp.where(filled[:, None] > 0, gathered, jnp.zeros_like(gathered))
    return kept_rows.reshape(experts, capacity, block_tokens.shape[1])


def hidden_units(inputs, gate_part, up_part):
    gate_value = jnp.dot(inputs, gate_part, preferred_element_type=jnp.float32)
    up_value = jnp.dot(inputs, up_part, preferred_element_type=jnp.float32)
    return (jax.nn.silu(gate_value) * up_value).astype(jnp.bfloat16)


def project_down(hidden, down_part):
    return lax.dot_general(
        hidden, down_part, (((1,), (1,)), ((), ())), preferred_element_type=jnp.float32
    )


def on_device(tokens, expert_ids, gate_weights, donor_group, gate_pieces, up_pieces, down_pieces):
    batches, local_rows, features = tokens.shape
    chosen = expert_ids.shape[2]
    experts = lax.axis_size("ep") // SPLIT
    capacity = local_rows * chosen * 5 // (4 * experts)
    tables = [
        slot_table(expert_ids[batch_index], experts, capacity) for batch_index in range(batches)
    ]
    packed = jnp.concatenate(
        [
            pack_rows(
                tokens[batch_index],
                tables[batch_index][1],
                tables[batch_index][2],
                experts,
                capacity,
            )
            for batch_index in range(batches)
        ],
        axis=1,
    )
    outgoing = jnp.repeat(packed, SPLIT, axis=0)
    arrived = lax.all_to_all(outgoing, "ep", split_axis=0, concat_axis=0, tiled=True)
    flat_rows = arrived.reshape(-1, features)
    hidden = hidden_units(flat_rows, gate_pieces[0], up_pieces[0])
    returned = lax.all_to_all(
        project_down(hidden, down_pieces[0]).astype(jnp.bfloat16).reshape(arrived.shape),
        "ep",
        split_axis=0,
        concat_axis=0,
        tiled=True,
    )
    expert_sums = jnp.sum(
        returned.reshape(experts, SPLIT, batches * capacity, features), axis=1, dtype=jnp.float32
    )
    results = []
    for batch_index in range(batches):
        block_out = expert_sums[:, batch_index * capacity : (batch_index + 1) * capacity].reshape(
            experts * capacity, features
        )
        picked = jnp.take(block_out, tables[batch_index][0], axis=0)
        weighted = jnp.sum(gate_weights[batch_index][:, :, None] * picked, axis=1)
        results.append(weighted.astype(jnp.bfloat16))
    mixed = jnp.stack(results, axis=0)
    span_rows = features // SECTIONS
    own_group = lax.axis_index("grp")
    own_slot = lax.axis_index("ep")
    slot_donors = lax.dynamic_index_in_dim(donor_group, own_slot, 1, keepdims=False)
    source_group = lax.dynamic_index_in_dim(slot_donors, own_group, 0, keepdims=False)
    own_rows = (gate_pieces[0, :span_rows], up_pieces[0, :span_rows], down_pieces[0, :span_rows])
    initial = tuple((jnp.zeros_like(member) for member in own_rows))
    carry = initial
    pieces = (
        lax.all_gather(own_rows[0], "grp", axis=0, tiled=True),
        lax.all_gather(own_rows[1], "grp", axis=0, tiled=True),
        lax.all_gather(own_rows[2], "grp", axis=0, tiled=True),
    )
    start = jnp.int32(0)
    count = pieces[0].shape[0] // span_rows
    for shard_index in range(count):
        position = start // span_rows + shard_index
        carry = tuple(
            (
                jnp.where(
                    position == source_group,
                    member[shard_index * span_rows : (shard_index + 1) * span_rows],
                    held,
                )
                for member, held in zip(pieces, carry)
            )
        )
    landed = jnp.stack(carry, axis=0)
    return (mixed, landed)


def solution(mesh):
    in_specs = (
        P(None, ("grp", "ep"), None),
        P(None, ("grp", "ep"), None),
        P(None, ("grp", "ep"), None),
        P(),
        P(("grp", "ep"), None, None),
        P(("grp", "ep"), None, None),
        P(("grp", "ep"), None, None),
    )
    out_specs = (P(None, ("grp", "ep"), None), P(None, ("grp", "ep"), None))
    return jax.shard_map(
        on_device, mesh=mesh, in_specs=in_specs, out_specs=out_specs, check_vma=False
    )
```

profile of v0, /device:TPU:91, one launch (start us, length us, event | category | flops | bytes accessed | tf_op | source)
XLA Modules:
  0.0 602.6 jit_solution(12120904134657537602)
XLA Ops:
  20.5 2.2 pad_maximum_fusion
  23.4 211.0 %all_to_all.10 = bf16[32,40,3584]{2,1,0:T(8,128)(2,1)S(1)} all-to-all(bf16[32,40,3584]{2,1,0:T(8,128)(2,1)S(1)} %bitcast.105), channel_id=1, replica_groups=mesh['grp'=8,'ep'=32] {'ep'}, dimensions={0} | all-to-all | bytes 18350080 | tf_op jit(solution)/shard_map/all_to_all | solution.py:65
  234.4 2.5 fusion.3
  237.0 2.6 fusion
  239.6 6.1 %convolution_convert_fusion = bf16[1280,3584]{1,0:T(8,128)(2,1)} fusion(bf16[1280,256]{1,0:T(8,128)(2,1)S(1)} %fusion, bf16[1,3584,256]{2,1,0:T(8,128)(2,1)S(1)} %copy-done.2), kind=kOutput, calls=%fused_computation.9 | convolution fusion | flops 2353397760 | bytes 11665408 | tf_op jit(solution)/shard_map/dot_general | solution.py:38
  245.8 7.9 %all-to-all-start.1 = ((bf16[32,40,3584]{2,1,0:T(8,128)(2,1)}), bf16[32,40,3584]{2,1,0:T(8,128)(2,1)}, u32[]{:S(2)}, u32[]{:S(2)}) async-start(bf16[32,40,3584]{2,1,0:T(8,128)(2,1)} %bitcast.104), calls=%async_computation.1 | async-start | bytes 18350080 | tf_op jit(solution)/shard_map/all_to_all | solution.py:68
  253.7 1.7 slice.113
  255.5 1.6 slice.122
  265.7 137.5 %all-gather.7.cloned.1.call-done = bf16[1,3584,256]{2,1,0:T(8,128)(2,1)} async-done(((bf16[1,448,256]{2,1,0:T(8,128)(2,1)}), bf16[1,3584,256]{2,1,0:T(8,128)(2,1)}) %all-gather.7.cloned.1.call-update) | async-done | bytes 1835024 | tf_op jit(solution)/shard_map/all_gather | solution.py:96
  403.2 1.6 fusion.31
  404.8 103.8 %all-gather.9.cloned.1.call-done = bf16[1,3584,256]{2,1,0:T(8,128)(2,1)} async-done(((bf16[1,448,256]{2,1,0:T(8,128)(2,1)}), bf16[1,3584,256]{2,1,0:T(8,128)(2,1)}) %all-gather.9.cloned.1.call-update) | async-done | bytes 1835024 | tf_op jit(solution)/shard_map/all_gather | solution.py:97
  508.6 1.6 fusion.32
  510.3 52.0 %all-gather.11.cloned.1.call-done = bf16[1,3584,256]{2,1,0:T(8,128)(2,1)} async-done(((bf16[1,448,256]{2,1,0:T(8,128)(2,1)}), bf16[1,3584,256]{2,1,0:T(8,128)(2,1)}) %all-gather.11.cloned.1.call-update) | async-done | bytes 1835024 | tf_op jit(solution)/shard_map/all_gather | solution.py:98
  562.3 1.6 fusion.33
  564.8 5.6 convert_reduce_fusion
  570.5 3.0 fusion.46
  573.5 1.9 reshape.151
  575.4 2.4 gather_fusion.2
  577.8 3.3 reshape.303
  581.1 1.9 reshape.152
  583.0 2.4 gather_fusion.3
  585.4 3.4 reshape.307
  588.9 3.1 fusion.6
  591.9 3.1 fusion.5
  (78 shorter events, 19.3 us)
Async XLA Ops:
  23.4 211.0 %copy-start.3 = (bf16[1,3584,256]{2,1,0:T(8,128)(2,1)S(1)}, bf16[1,3584,256]{2,1,0:T(8,128)(2,1)}, u32[]{:S(2)}) copy-start(bf16[1,3584,256]{2,1,0:T(8,128)(2,1)} %param.15) | copy-start | bytes 5505028
  234.4 2.6 copy-start.4
  237.0 2.6 copy-start.2
  245.8 319.1 %all-to-all-start.1 = ((bf16[32,40,3584]{2,1,0:T(8,128)(2,1)}), bf16[32,40,3584]{2,1,0:T(8,128)(2,1)}, u32[]{:S(2)}, u32[]{:S(2)}) async-start(bf16[32,40,3584]{2,1,0:T(8,128)(2,1)} %bitcast.104), calls=%async_computation.1 | async-start | bytes 18350080 | tf_op jit(solution)/shard_map/all_to_all | solution.py:68
  253.7 4.7 copy-start.5
  253.7 5.1 copy-start.6
  253.7 149.5 %all-gather.7.cloned.1.call-start = ((), (), s32[]{:S(2)}) async-start(), calls=%async_computation.2 | async-start | bytes 2064384 | tf_op jit(solution)/shard_map/all_gather | solution.py:96
  255.4 253.2 %all-gather.9.cloned.1.call-start = ((), (), s32[]{:S(2)}) async-start(), calls=%async_computation.3 | async-start | bytes 2064384 | tf_op jit(solution)/shard_map/all_gather | solution.py:97
  257.1 305.1 %all-gather.11.cloned.1.call-start = ((), (), s32[]{:S(2)}) async-start(), calls=%async_computation.4 | async-start | bytes 2064384 | tf_op jit(solution)/shard_map/all_gather | solution.py:98
  585.4 3.4 copy-start
  588.9 3.1 copy-start.1
Sparse Core Ops, SparseCore 0:
  256.3 146.8 all-gather.6
  405.5 103.0 all-gather.8
  511.0 51.2 all-gather.10
where the time goes:
time: 607 us; the launch traced here: 603 us
  waiting for transfers between devices  293 us (48%)
  blocking collectives  211 us (35%)
  local copies, waits for them, and re-layouts  36.8 us (6%)
  other arithmetic  23 us (4%)
  between operations  19.2 us (3%)
  matrix products  11.3 us (2%)
  starting transfers between devices  8.02 us (1%)
    all_to_all x1, blocking collectives, on_device(): lax.all_to_all(outgoing, 'ep', split_axis=0, concat_axis=0, tiled=True)  211 us
    all_gather x1, waiting for transfers between devices, on_device(): lax.all_gather(own_rows[0], 'grp', axis=0, tiled=True)  137 us
    all_gather x1, waiting for transfers between devices, on_device(): lax.all_gather(own_rows[1], 'grp', axis=0, tiled=True)  104 us
    all_gather x1, waiting for transfers between devices, on_device(): lax.all_gather(own_rows[2], 'grp', axis=0, tiled=True)  52 us
  transfers between devices with their start and end apart: 4, of which 3 were waited for; matrix products, arithmetic and copies ran while one was open for 2% of the time, Pallas kernels for 0%

commit v1 on v0

v1 whole, which is shorter than its diff:
```python
import jax
import jax.numpy as jnp
from jax import lax
from jax.experimental import pallas as pl
from jax.experimental.pallas import tpu as pltpu
from jax.sharding import PartitionSpec as P

MESH = pl.DeviceIdType.MESH
D = 3584
F = 256
CAP = 20
HALF = 40
CH = 80
TILE = 512
SPAN = 448
BF = jnp.bfloat16
F32 = jnp.float32


def rows(index, size=CH):
    return pl.ds(pl.multiple_of(index * size, 16), size)


def layer(
    tok_ref, meta_ref, donor_ref, gate_ref, up_ref, down_ref, mixed_ref, landed_ref,
    tok_all, meta_all, onehot, w_hi, w_lo, pack, zin, xin, gw, uw, dw, gacc, uacc, hid,
    part, c1buf, c2buf, zout, zback, acc, ex_send, ex_recv, cand, lsend, lrecv,
    load_sem, s_send, s_recv, z_send, z_recv, x_send, x_recv, r_send,
    c1_send, c1_recv, c2_send, c2_recv, c3_send, zo_recv, b_send, b_recv,
    y_send, y_recv, l_send, l_recv,
):
    grp = lax.axis_index("grp")
    ep = lax.axis_index("ep")
    y, zl = grp // 2, grp % 2
    z, x, c = ep // 8, (ep // 2) % 4, ep % 2
    pair = x // 2
    mate = x + 1 - 2 * (x % 2)
    cross = (x + 2) % 4

    def at(zz, xx, cc):
        return (grp, zz * 8 + xx * 2 + cc)

    sibling = at(z, x, 1 - c)

    def ygroup(d):
        return (((y + d) % 4) * 2 + zl, ep)

    partner = (y * 2 + 1 - zl, ep)

    def remote(src, dst, send, recv, target):
        return pltpu.make_async_remote_copy(
            src_ref=src, dst_ref=dst, send_sem=send, recv_sem=recv,
            device_id=target, device_id_type=MESH,
        )

    pieces = (gate_ref, up_ref, down_ref)
    loads = [
        pltpu.make_async_copy(tok_ref, tok_all.at[pl.ds(0, 128)], load_sem.at[0]),
        pltpu.make_async_copy(gate_ref, gw, load_sem.at[1]),
        pltpu.make_async_copy(up_ref, uw, load_sem.at[2]),
        pltpu.make_async_copy(down_ref, dw, load_sem.at[3]),
    ] + [
        pltpu.make_async_copy(pieces[j].at[pl.ds(0, SPAN)], cand.at[j], load_sem.at[4 + j])
        for j in range(3)
    ]
    for cp in loads:
        cp.start()

    barrier = pltpu.get_barrier_semaphore()
    greeted = [at(z, (x + i) % 4, c) for i in range(1, 4)]
    greeted += [at(z, (x + i) % 4, 1 - c) for i in range(4)]
    greeted += [at((z + i) % 4, x, c) for i in range(1, 4)]
    greeted += [ygroup(i) for i in range(1, 4)]
    greeted += [partner]
    for target in greeted:
        pl.semaphore_signal(barrier, inc=1, device_id=target, device_id_type=MESH)
    pl.semaphore_wait(barrier, len(greeted))

    sib_meta = remote(meta_ref, meta_all, s_send.at[1], s_recv.at[1], sibling)
    sib_meta.start()
    sib_tok = remote(tok_ref, tok_all.at[pl.ds(128, 128)], s_send.at[0], s_recv.at[0], sibling)
    sib_tok.start()
    y_copies = []
    for k, d in enumerate((1, 3, 2)):
        for j in range(3):
            cp = remote(
                pieces[j].at[pl.ds(0, SPAN)], cand.at[((4 - d) % 4) * 3 + j],
                y_send.at[k * 3 + j], y_recv.at[(d - 1) * 3 + j], ygroup(d),
            )
            cp.start()
            y_copies.append(cp)

    sib_meta.wait_recv()
    row8 = lax.broadcasted_iota(jnp.int32, (8, 128), 0)
    lane8 = lax.broadcasted_iota(jnp.int32, (8, 128), 1)
    expert = (2 * ((row8 + z) % 4) + c).astype(F32)
    first = lax.broadcasted_iota(jnp.int32, (128, 128), 0)
    second = lax.broadcasted_iota(jnp.int32, (128, 128), 1)
    before = jnp.where((first < second) & (first // 64 == second // 64), 1.0, 0.0).astype(BF)
    slot = lax.broadcasted_iota(jnp.int32, (CH, 128), 0).astype(F32)
    for h, meta in enumerate((meta_ref, meta_all)):
        id0, id1 = meta[0:1, :], meta[1:2, :]
        w0, w1 = meta[2:3, :], meta[3:4, :]
        hit0, hit1 = expert == id0, expert == id1
        named = jnp.where(hit0 | hit1, 1.0, 0.0)
        rank = jnp.dot(named.astype(BF), before, preferred_element_type=F32)
        place = rank + jnp.where(lane8 >= 64, float(CAP), 0.0) + float(HALF * h)
        place = jnp.where(named > 0.0, place, -1.0)
        weight = jnp.where(hit0, w0, jnp.where(hit1, w1, 0.0))
        for d in range(4):
            match = place[d : d + 1, :] == slot
            ww = jnp.where(match, weight[d : d + 1, :], 0.0)
            hi = ww.astype(BF)
            onehot[pl.ds(d * CH, CH), pl.ds(h * 128, 128)] = jnp.where(match, 1.0, 0.0).astype(BF)
            w_hi[pl.ds(d * CH, CH), pl.ds(h * 128, 128)] = hi
            w_lo[pl.ds(d * CH, CH), pl.ds(h * 128, 128)] = (ww - hi.astype(F32)).astype(BF)

    loads[0].wait()
    sib_tok.wait_recv()

    def tiles(body):
        def step(i, carry):
            body(pl.ds(pl.multiple_of(i * TILE, TILE), TILE))
            return carry

        lax.fori_loop(0, D // TILE, step, 0)

    def pack_chunk(d):
        def body(cols):
            pack[pl.ds(d * CH, CH), cols] = jnp.dot(
                onehot[pl.ds(d * CH, CH), :], tok_all[:, cols], preferred_element_type=F32
            ).astype(BF)

        tiles(body)

    def z_copy(d):
        return remote(
            pack.at[pl.ds(d * CH, CH)], zin.at[pl.ds((d - 1) * CH, CH)],
            z_send.at[d - 1], z_recv.at[d - 1], at((z + d) % 4, x, c),
        )

    z_copies = {d: z_copy(d) for d in (1, 2, 3)}
    for d in (1, 3):
        pack_chunk(d)
        z_copies[d].start()
    pack_chunk(0)

    serve = 1 - (pair + c) % 2

    def fan(q):
        src = pack.at[pl.ds(0, CH)] if q == 0 else zin.at[pl.ds((q - 1) * CH, CH)]
        dst = xin.at[rows(q * 4 + x)]
        f = (q + x) % 2
        t0 = at(z, serve * mate + (1 - serve) * (2 * c), f)
        t1 = at(
            z, serve * x + (1 - serve) * (2 * c + 1), serve * (1 - c) + (1 - serve) * f
        )
        return (
            remote(src, dst, x_send.at[q * 2], x_recv.at[q * 4 + x], t0),
            remote(src, dst, x_send.at[q * 2 + 1], x_recv.at[q * 4 + x], t1),
            pltpu.make_async_copy(src, dst, x_recv.at[q * 4 + x]),
        )

    def fan_start(q):
        first_copy, second_copy, local = fan(q)
        first_copy.start()
        second_copy.start()

        @pl.when(serve == 1)
        def _():
            local.start()

    def even(q):
        return 1 - (x + c + q) % 2

    def x_wait(q, xs):
        ref = xin.at[rows(q * 4 + xs)]
        pltpu.make_async_copy(ref, ref, x_recv.at[q * 4 + xs]).wait()

    def relay(q, xs):
        ref = xin.at[rows(q * 4 + xs)]
        return remote(ref, ref, r_send.at[q * 4 + xs], x_recv.at[q * 4 + xs], sibling)

    def fan_recv(q):
        x1, x2, x3 = (x + 1) % 4, (x + 2) % 4, (x + 3) % 4

        @pl.when(even(q) == 1)
        def _():
            x_wait(q, x2)
            relay(q, x2).start()
            x_wait(q, x1)
            x_wait(q, x3)

        @pl.when(even(q) == 0)
        def _():
            x_wait(q, x1)
            relay(q, x1).start()
            x_wait(q, x3)
            relay(q, x3).start()
            x_wait(q, x2)

        x_wait(q, x)

    def compute(q):
        r = pl.ds(q * 4 * CH, 4 * CH)
        gacc[...] = jnp.zeros_like(gacc)
        uacc[...] = jnp.zeros_like(uacc)

        def up_body(cols):
            a = xin[r, cols]
            gacc[...] += jnp.dot(a, gw[cols, :], preferred_element_type=F32)
            uacc[...] += jnp.dot(a, uw[cols, :], preferred_element_type=F32)

        tiles(up_body)
        g = gacc[...]
        hid[...] = (g / (1.0 + jnp.exp(-g)) * uacc[...]).astype(BF)

        def down_body(cols):
            part[r, cols] = lax.dot_general(
                hid[...], dw[cols, :], (((1,), (1,)), ((), ())), preferred_element_type=F32
            ).astype(BF)

        tiles(down_body)

    def keep_of(q, own):
        u = even(q) if own else 1 - even(q)
        return u * x + (1 - u) * (3 - x)

    def send_of(q, own):
        u = even(q) if own else 1 - even(q)
        return u * cross + (1 - u) * mate

    def c1(q):
        return (
            remote(
                part.at[rows(q * 4 + send_of(q, False))], c1buf.at[pl.ds((q * 2 + 1) * CH, CH)],
                c1_send.at[q * 2 + 1], c1_recv.at[q * 2 + 1], sibling,
            ),
            remote(
                part.at[rows(q * 4 + keep_of(q, False))], c1buf.at[pl.ds(q * 2 * CH, CH)],
                c1_send.at[q * 2], c1_recv.at[q * 2], sibling,
            ),
        )

    def c1_start(q):
        for cp in c1(q):
            cp.start()

    def c2(q):
        return remote(
            part.at[rows(q * 4 + send_of(q, True))], c2buf.at[pl.ds(q * CH, CH)],
            c2_send.at[q], c2_recv.at[q], at(z, mate, c),
        )

    def add_rows(base, buffers):
        def step(i, carry):
            here = pl.ds(pl.multiple_of(base + i * 16, 16), 16)
            total = part[here, :].astype(F32)
            for buf, offset in buffers:
                total += buf[pl.ds(pl.multiple_of(offset + i * 16, 16), 16), :].astype(F32)
            part[here, :] = total.astype(BF)
            return carry

        lax.fori_loop(0, CH // 16, step, 0)

    def c2_start(q):
        c1(q)[0].wait_recv()
        add_rows((q * 4 + send_of(q, True)) * CH, [(c1buf, (q * 2 + 1) * CH)])
        c2(q).start()

    def c3(q):
        src, dst = part.at[rows(q * 4 + keep_of(q, True))], zout.at[pl.ds(q * CH, CH)]
        u = even(q)
        return (
            remote(
                src, dst, c3_send.at[q], zo_recv.at[q], at(z, u * x + (1 - u) * (3 - x), pair)
            ),
            pltpu.make_async_copy(src, dst, zo_recv.at[q]),
            u * serve,
        )

    def c3_start(q):
        c1(q)[1].wait_recv()
        c2(q).wait_recv()
        add_rows(
            (q * 4 + keep_of(q, True)) * CH, [(c1buf, q * 2 * CH), (c2buf, q * CH)]
        )
        away, local, here = c3(q)

        @pl.when(here == 1)
        def _():
            local.start()

        @pl.when(here == 0)
        def _():
            away.start()

    def zout_wait(q):
        ref = zout.at[pl.ds(q * CH, CH)]
        pltpu.make_async_copy(ref, ref, zo_recv.at[q]).wait()

    def back(q):
        return remote(
            zout.at[pl.ds(q * CH, CH)], zback.at[pl.ds((q - 1) * CH, CH)],
            b_send.at[q - 1], b_recv.at[q - 1], at((z + 4 - q) % 4, x, c),
        )

    def mix(q, start):
        src, base = (zout, 0) if q == 0 else (zback, (q - 1) * CH)
        dims = (((0,), (0,)), ((), ()))

        def body(cols):
            b = src[pl.ds(base, CH), cols]
            r = pl.ds(q * CH, CH)
            value = lax.dot_general(w_hi[r, :], b, dims, preferred_element_type=F32)
            value += lax.dot_general(w_lo[r, :], b, dims, preferred_element_type=F32)
            acc[:, cols] = value if start else acc[:, cols] + value

        tiles(body)

    fan_start(0)
    pack_chunk(2)
    for k in (1, 2, 3):
        loads[k].wait()
    fan_recv(0)
    compute(0)
    c1_start(0)
    c2_start(0)
    for d in (1, 3):
        z_copies[d].wait_send()
    z_copies[2].start()
    for q in (1, 3):
        z_copies[q].wait_recv()
        fan_start(q)
    c3_start(0)

    for j in range(3):
        loads[4 + j].wait()
    for cp in y_copies:
        cp.wait_send()
    for d in (1, 2, 3):
        for j in range(3):
            ref = cand.at[((4 - d) % 4) * 3 + j]
            pltpu.make_async_copy(ref, ref, y_recv.at[(d - 1) * 3 + j]).wait()
    asked = donor_ref[y * 2 + 1 - zl, ep]
    asked_y = (asked // 2 + 4 - y) % 4
    for j in range(3):
        lsend[j] = cand[asked_y * 3 + j]
    l_copy = remote(lsend, lrecv, l_send, l_recv, partner)

    for q in (1, 3):
        fan_recv(q)
        compute(q)
        c1_start(q)
    for q in (1, 3):
        c2_start(q)
    z_copies[2].wait_recv()
    fan_start(2)
    l_copy.start()
    for q in (1, 3):
        c3_start(q)
    zout_wait(0)
    mix(0, True)
    for q in (1, 3):
        zout_wait(q)
        back(q).start()
    fan_recv(2)
    compute(2)
    c1_start(2)
    c2_start(2)
    c3_start(2)
    zout_wait(2)
    back(2).start()
    l_copy.wait()
    wanted = donor_ref[grp, ep]
    wanted_y = (wanted // 2 + 4 - y) % 4
    wanted_z = wanted % 2
    for j in range(3):
        near = cand[wanted_y * 3 + j].astype(F32)
        far = lrecv[j].astype(F32)
        from_here = jnp.full((SPAN, F), wanted_z, jnp.int32) == zl
        landed_ref[j] = jnp.where(from_here, near, far).astype(BF)
    for q in (1, 3, 2):
        back(q).wait_recv()
        mix(q, False)

    def cut(cols):
        ex_send[:, cols] = acc[pl.ds(128, 128), cols].astype(BF)

    tiles(cut)
    swap = remote(ex_send, ex_recv, s_send.at[2], s_recv.at[2], sibling)
    swap.start()
    swap.wait()

    def join(cols):
        mixed_ref[:, cols] = (
            acc[pl.ds(0, 128), cols] + ex_recv[:, cols].astype(F32)
        ).astype(BF)

    tiles(join)

    sib_meta.wait_send()
    sib_tok.wait_send()
    z_copies[2].wait_send()
    for q in range(4):
        first_copy, second_copy, _ = fan(q)
        first_copy.wait_send()
        second_copy.wait_send()

        @pl.when(even(q) == 1)
        def _():
            relay(q, (x + 2) % 4).wait_send()

        @pl.when(even(q) == 0)
        def _():
            relay(q, (x + 1) % 4).wait_send()
            relay(q, (x + 3) % 4).wait_send()

        for cp in c1(q):
            cp.wait_send()
        c2(q).wait_send()
        away, _, here = c3(q)

        @pl.when(here == 0)
        def _():
            away.wait_send()

        if q:
            back(q).wait_send()


def on_device(tokens, expert_ids, gate_weights, donor_group, gate_pieces, up_pieces, down_pieces):
    tok = tokens.reshape(128, D)
    ids = expert_ids.reshape(128, 2).T.astype(F32)
    wts = gate_weights.reshape(128, 2).T
    meta = jnp.concatenate([ids, wts, jnp.zeros((4, 128), F32)], axis=0)
    vmem, hbm = pltpu.VMEM, pl.ANY
    dma = pltpu.SemaphoreType.DMA
    mixed, landed = pl.pallas_call(
        layer,
        out_shape=(
            jax.ShapeDtypeStruct((128, D), BF),
            jax.ShapeDtypeStruct((3, SPAN, F), BF),
        ),
        in_specs=[
            pl.BlockSpec(memory_space=hbm),
            pl.BlockSpec(memory_space=vmem),
            pl.BlockSpec(memory_space=pltpu.SMEM),
            pl.BlockSpec(memory_space=hbm),
            pl.BlockSpec(memory_space=hbm),
            pl.BlockSpec(memory_space=hbm),
        ],
        out_specs=(pl.BlockSpec(memory_space=vmem), pl.BlockSpec(memory_space=vmem)),
        scratch_shapes=[
            vmem((256, D), BF),
            vmem((8, 128), F32),
            vmem((4 * CH, 256), BF),
            vmem((4 * CH, 256), BF),
            vmem((4 * CH, 256), BF),
            vmem((4 * CH, D), BF),
            vmem((3 * CH, D), BF),
            vmem((16 * CH, D), BF),
            vmem((D, F), BF),
            vmem((D, F), BF),
            vmem((D, F), BF),
            vmem((4 * CH, F), F32),
            vmem((4 * CH, F), F32),
            vmem((4 * CH, F), BF),
            vmem((16 * CH, D), BF),
            vmem((8 * CH, D), BF),
            vmem((4 * CH, D), BF),
            vmem((4 * CH, D), BF),
            vmem((3 * CH, D), BF),
            vmem((256, D), F32),
            vmem((128, D), BF),
            vmem((128, D), BF),
            vmem((12, SPAN, F), BF),
            vmem((3, SPAN, F), BF),
            vmem((3, SPAN, F), BF),
            dma((7,)),
            dma((3,)), dma((3,)),
            dma((3,)), dma((3,)),
            dma((8,)), dma((16,)), dma((16,)),
            dma((8,)), dma((8,)),
            dma((4,)), dma((4,)),
            dma((4,)), dma((4,)),
            dma((3,)), dma((3,)),
            dma((9,)), dma((9,)),
            dma, dma,
        ],
        compiler_params=pltpu.CompilerParams(
            collective_id=0, has_side_effects=True, vmem_limit_bytes=62 * 2**20
        ),
        cost_estimate=pl.CostEstimate(
            flops=8 * 10**9, bytes_accessed=10**7, transcendentals=4 * 10**5
        ),
    )(tok, meta, donor_group, gate_pieces[0], up_pieces[0], down_pieces[0])
    return mixed.reshape(2, 64, D), landed


def solution(mesh):
    in_specs = (
        P(None, ("grp", "ep"), None),
        P(None, ("grp", "ep"), None),
        P(None, ("grp", "ep"), None),
        P(),
        P(("grp", "ep"), None, None),
        P(("grp", "ep"), None, None),
        P(("grp", "ep"), None, None),
    )
    out_specs = (P(None, ("grp", "ep"), None), P(None, ("grp", "ep"), None))
    return jax.shard_map(
        on_device, mesh=mesh, in_specs=in_specs, out_specs=out_specs, check_vma=False
    )
```

time: 607 us -> 189 us (0.31)
  waiting for transfers between devices: 293 us -> 0 us
  blocking collectives: 211 us -> 0 us
  Pallas kernels: 0 us -> 180 us
  local copies, waits for them, and re-layouts: 36.8 us -> 4.01 us
  other arithmetic: 23 us -> 1.34 us
  between operations: 19.2 us -> 0.66 us
  matrix products: 11.3 us -> 0 us
  starting transfers between devices: 8.02 us -> 0 us
    all_gather x3 -> x0, waiting for transfers between devices: 293 us -> none  [the longest x1 137 us: on_device(): lax.all_gather(own_rows[0], 'grp', axis=0, tiled=True)]
    all_to_all x1 -> x0, blocking collectives: 211 us -> none  [on_device(): lax.all_to_all(outgoing, 'ep', split_axis=0, concat_axis=0, tiled=True)]
    pallas_call x0 -> x1, Pallas kernels: none -> 180 us  [on_device(): pl.pallas_call(layer, out_shape=(jax.ShapeDtypeStruct((128, D), BF), jax....]
    gather x6 -> x0, local copies, waits for them, and re-layouts: 14.1 us -> none  [the longest x4 11.5 us: on_device(): picked = jnp.take(block_out, tables[batch_index][0], axis=0)]
    reduce_sum x5 -> x0, other arithmetic: 12.2 us -> none  [the longest x2 6.19 us: on_device(): weighted = jnp.sum(gate_weights[batch_index][:, :, None] * picked, axis=1)]
    dot_general x3 -> x0, matrix products: 11.3 us -> none  [the longest x1 6.14 us: project_down(): lax.dot_general(hidden, down_part, (((1,), (1,)), ((), ())), preferred_el...]
    all_to_all x1 -> x0, starting transfers between devices: 7.9 us -> none  [on_device(): lax.all_to_all(project_down(hidden, down_pieces[0]).astype(jnp.bfloat16)....]
    slice x6 -> x0, local copies, waits for them, and re-layouts: 7.24 us -> none  [the longest x1 3.04 us: on_device(): expert_sums[:, batch_index * capacity:(batch_index + 1) * capacity]]
  transfers between devices with their start and end apart: 4 -> 0, of which waited for: 3 -> 0; matrix products, arithmetic and copies ran while one was open for 2% -> 0% of each run, Pallas kernels for 0% -> 0%
where the time goes in v1:
time: 189 us; the launch traced here: 186 us
  Pallas kernels  180 us (95%)
  local copies, waits for them, and re-layouts  4.01 us (2%)
    pallas_call x1, Pallas kernels, on_device(): pl.pallas_call(layer, out_shape=(jax.ShapeDtypeStruct((128, D), BF), jax....  180 us

profile of v1, /device:TPU:91, one launch (start us, length us, event | category | flops | bytes accessed | tf_op | source)
XLA Modules:
  0.0 185.8 jit_solution(8190566913682001700)
XLA Ops:
  0.6 0.1 pad.2.clone
  0.7 0.7 convert_element_type.9
  1.4 0.1 convert_element_type.10
  1.5 0.7 copy.10
  2.2 0.1 reshape.16
  2.3 0.7 maximum_maximum_fusion.meta_ref
  2.9 179.8 %shard_map.86 = (bf16[128,3584]{1,0:T(8,128)(2,1)}, bf16[3,448,256]{2,1,0:T(8,128)(2,1)}) custom-call(bf16[128,3584]{1,0:T(8,128)(2,1)} %bitcast.17, f32[8,128]{1,0:T(8,128)} %maximum_maximum_fusion.meta_ref, s32[8,32]{1,0:T(8,128)} %donor_ref.1, bf16[3584,256]{1,0:T(8,128)(2,1)} %bitcast.14, bf16[3584,256]{1,0:T(8,128)(2,1)} %bitcast.15, ...), custom_call_target="tpu_custom_call" | custom-call | flops 8000000000 | bytes 10000000 | tf_op jit(solution)/shard_map/pallas_call | solution.py:439
  182.7 0.0 copy-start
  182.7 2.2 %copy.13 = bf16[2,64,3584]{2,1,0:T(8,128)(2,1)} copy(bf16[2,64,3584]{2,1,0:T(8,128)(2,1)} %bitcast.11) | data formatting | bytes 1835008
  185.0 0.0 copy-done
  185.0 0.8 copy.14
  (2 shorter events, 0.0 us)
Async XLA Ops:
  182.7 2.2 %copy-start = (bf16[3,448,256]{2,1,0:T(8,128)(2,1)S(1)}, bf16[3,448,256]{2,1,0:T(8,128)(2,1)}, u32[]{:S(2)}) copy-start(bf16[3,448,256]{2,1,0:T(8,128)(2,1)} %get-tuple-element.9) | copy-start | bytes 2064388

commit v2 on v1

v2 whole, which is shorter than its diff:
```python
import jax
import jax.numpy as jnp
from jax import lax
from jax.experimental import pallas as pl
from jax.experimental.pallas import tpu as pltpu
from jax.sharding import PartitionSpec as P

MESH = pl.DeviceIdType.MESH
D = 3584
F = 256
CAP = 20
HALF = 40
CH = 80
K = 2
WIDE = D // K
TILE = 896
LEN = (48, 32)
OFF = (0, 48)
SPAN = 448
BF = jnp.bfloat16
F32 = jnp.float32


def rows(index, size=CH):
    return pl.ds(pl.multiple_of(index * size, 16), size)


def layer(
    tok_ref, meta_ref, donor_ref, gate_ref, up_ref, down_ref, mixed_ref, landed_ref,
    tok_all, meta_all, onehot, weight_t, pack, zin, xin, gw, uw, dw, gacc, uacc, hid,
    part, c1buf, c2buf, zout, home, acc, ex_send, ex_recv, cand, lsend, lrecv,
    load_sem, m_send, m_recv, t_send, t_recv, z_send, z_recv, x_send, x_recv, r_send,
    c1_send, c1_recv, c2_send, c2_recv, c3_send, zo_recv, b_send, b_recv,
    y_send, y_recv, l_send, l_recv, e_send, e_recv,
):
    grp = lax.axis_index("grp")
    ep = lax.axis_index("ep")
    y, zl = grp // 2, grp % 2
    z, x, c = ep // 8, (ep // 2) % 4, ep % 2
    pair = x // 2
    mate = x + 1 - 2 * (x % 2)
    cross = (x + 2) % 4
    near = 3 - x
    serve = 1 - (pair + c) % 2

    def at(zz, xx, cc):
        return (grp, zz * 8 + xx * 2 + cc)

    sibling = at(z, x, 1 - c)

    def ygroup(d):
        return (((y + d) % 4) * 2 + zl, ep)

    partner = (y * 2 + 1 - zl, ep)

    def remote(src, dst, send, recv, target):
        return pltpu.make_async_remote_copy(
            src_ref=src, dst_ref=dst, send_sem=send, recv_sem=recv,
            device_id=target, device_id_type=MESH,
        )

    def arrived(ref, sem):
        pltpu.make_async_copy(ref, ref, sem).wait()

    def piece(k):
        return pl.ds(k * WIDE, WIDE)

    def chunk(q, r, sides=1):
        return pl.ds(sides * (q * CH + OFF[r]), sides * LEN[r])

    def side(q, r, sides, i):
        base = sides * (q * CH + OFF[r])
        return pl.ds(pl.multiple_of(base + i * LEN[r], 16), LEN[r])

    pieces = (gate_ref, up_ref, down_ref)
    loads = [
        pltpu.make_async_copy(tok_ref, tok_all.at[pl.ds(0, 128)], load_sem.at[0]),
        pltpu.make_async_copy(gate_ref, gw, load_sem.at[1]),
        pltpu.make_async_copy(up_ref, uw, load_sem.at[2]),
        pltpu.make_async_copy(down_ref, dw, load_sem.at[3]),
    ] + [
        pltpu.make_async_copy(pieces[j].at[pl.ds(0, SPAN)], cand.at[j], load_sem.at[4 + j])
        for j in range(3)
    ]
    for cp in loads:
        cp.start()

    barrier = pltpu.get_barrier_semaphore()
    greeted = [at(z, x, 1 - c)]
    greeted += [at(z, (x + i) % 4, c) for i in range(1, 4)]
    greeted += [at(z, (x + i) % 4, 1 - c) for i in range(1, 4)]
    greeted += [at((z + i) % 4, x, c) for i in range(1, 4)]
    greeted += [ygroup(i) for i in range(1, 4)]
    greeted += [partner]
    for target in greeted:
        pl.semaphore_signal(barrier, inc=1, device_id=target, device_id_type=MESH)
    pl.semaphore_wait(barrier, len(greeted))

    sib_meta = remote(meta_ref, meta_all, m_send, m_recv, sibling)
    sib_meta.start()

    def sib_tok(k):
        return remote(
            tok_ref.at[:, piece(k)], tok_all.at[pl.ds(128, 128), piece(k)],
            t_send.at[k], t_recv.at[k], sibling,
        )

    for k in range(K):
        sib_tok(k).start()
    y_copies = []
    for n, d in enumerate((1, 3, 2)):
        for j in range(3):
            cp = remote(
                pieces[j].at[pl.ds(0, SPAN)], cand.at[((4 - d) % 4) * 3 + j],
                y_send.at[n * 3 + j], y_recv.at[(d - 1) * 3 + j], ygroup(d),
            )
            cp.start()
            y_copies.append(cp)

    sib_meta.wait_recv()
    row8 = lax.broadcasted_iota(jnp.int32, (8, 128), 0)
    lane8 = lax.broadcasted_iota(jnp.int32, (8, 128), 1)
    expert = (2 * ((row8 + z) % 4) + c).astype(F32)
    first = lax.broadcasted_iota(jnp.int32, (128, 128), 0)
    second = lax.broadcasted_iota(jnp.int32, (128, 128), 1)
    before = jnp.where((first < second) & (first // 64 == second // 64), 1.0, 0.0).astype(BF)
    slot = lax.broadcasted_iota(jnp.int32, (CH, 128), 0).astype(F32)
    for h, meta in enumerate((meta_ref, meta_all)):
        id0, id1 = meta[0:1, :], meta[1:2, :]
        w0, w1 = meta[2:3, :], meta[3:4, :]
        hit0, hit1 = expert == id0, expert == id1
        named = jnp.where(hit0 | hit1, 1.0, 0.0)
        rank = jnp.dot(named.astype(BF), before, preferred_element_type=F32)
        place = rank + jnp.where(lane8 >= 64, float(CAP), 0.0) + float(HALF * h)
        place = jnp.where(named > 0.0, place, -1.0)
        weight = jnp.where(hit0, w0, jnp.where(hit1, w1, 0.0))
        for d in range(4):
            match = place[d : d + 1, :] == slot
            here = (pl.ds(d * CH, CH), pl.ds(h * 128, 128))
            onehot[here] = jnp.where(match, 1.0, 0.0).astype(BF)
            weight_t[here] = jnp.where(match, weight[d : d + 1, :], 0.0).astype(BF)

    loads[0].wait()

    def tiles(body, start=0, size=D):
        def step(i, carry):
            body(pl.ds(pl.multiple_of(start + i * TILE, 128), TILE))
            return carry

        lax.fori_loop(0, size // TILE, step, 0)

    def pack_chunk(d, k):
        def body(cols):
            pack[pl.ds(d * CH, CH), cols] = jnp.dot(
                onehot[pl.ds(d * CH, CH), :], tok_all[:, cols], preferred_element_type=F32
            ).astype(BF)

        tiles(body, k * WIDE, WIDE)

    def z_copy(d, r):
        n = (d - 1) * 2 + r
        return remote(
            pack.at[chunk(d, r)], zin.at[chunk(d - 1, r)],
            z_send.at[n], z_recv.at[n], at((z + d) % 4, x, c),
        )

    def fan(q, r):
        src = pack.at[chunk(0, r)]
        if q:
            src = zin.at[chunk(q - 1, r)]
        dst = xin.at[side(q, r, 4, x)]
        f = (q // 2 + x + r) % 2
        n = q * 2 + r
        recv = x_recv.at[n * 4 + x]
        t0 = at(z, serve * mate + (1 - serve) * near, f)
        return (
            remote(src, dst, x_send.at[n * 2], recv, t0),
            remote(src, dst, x_send.at[n * 2 + 1], recv, sibling),
            pltpu.make_async_copy(src, dst, recv),
            remote(src, dst, x_send.at[n * 2 + 1], recv, at(z, cross, f)),
        )

    def fan_start(q, r):
        away, over, local, beyond = fan(q, r)
        away.start()

        @pl.when(serve == 1)
        def _():
            over.start()
            local.start()

        @pl.when(serve == 0)
        def _():
            beyond.start()

    def even(q, r):
        return 1 - (x + c + q // 2 + r) % 2

    def x_wait(q, r, xs):
        arrived(xin.at[side(q, r, 4, xs)], x_recv.at[(q * 2 + r) * 4 + xs])

    def relay(q, r, xs):
        ref = xin.at[side(q, r, 4, xs)]
        n = (q * 2 + r) * 4 + xs
        return remote(ref, ref, r_send.at[n], x_recv.at[n], sibling)

    def relay_near(q, r):
        @pl.when(even(q, r) == 0)
        def _():
            x_wait(q, r, near)
            relay(q, r, near).start()

    def relay_rest(q, r):
        @pl.when(even(q, r) == 0)
        def _():
            x_wait(q, r, mate)
            relay(q, r, mate).start()

        @pl.when(even(q, r) == 1)
        def _():
            x_wait(q, r, cross)
            relay(q, r, cross).start()

    def up(q, r):
        @pl.when(even(q, r) == 0)
        def _():
            x_wait(q, r, cross)

        @pl.when(even(q, r) == 1)
        def _():
            x_wait(q, r, near)
            x_wait(q, r, mate)

        x_wait(q, r, x)
        o = chunk(q, r, 4)
        s = pl.ds(0, 4 * LEN[r])
        gacc[s, :] = jnp.zeros((4 * LEN[r], F), F32)
        uacc[s, :] = jnp.zeros((4 * LEN[r], F), F32)

        def body(cols):
            a = xin[o, cols]
            gacc[s, :] += jnp.dot(a, gw[cols, :], preferred_element_type=F32)
            uacc[s, :] += jnp.dot(a, uw[cols, :], preferred_element_type=F32)

        tiles(body)
        g = gacc[s, :]
        hid[o, :] = (g / (1.0 + jnp.exp(-g)) * uacc[s, :]).astype(BF)

    def keep_of(q, r, own):
        u = even(q, r) if own else 1 - even(q, r)
        return u * x + (1 - u) * near

    def send_of(q, r, own):
        u = even(q, r) if own else 1 - even(q, r)
        return u * cross + (1 - u) * mate

    def c1(q, r):
        n = (q * 2 + r) * 2
        return (
            remote(
                part.at[side(q, r, 4, send_of(q, r, False))],
                c1buf.at[side(q, r, 2, 1)],
                c1_send.at[n + 1], c1_recv.at[n + 1], sibling,
            ),
            remote(
                part.at[side(q, r, 4, keep_of(q, r, False))],
                c1buf.at[side(q, r, 2, 0)],
                c1_send.at[n], c1_recv.at[n], sibling,
            ),
        )

    def down(q, r):
        o = chunk(q, r, 4)

        def body(cols):
            part[o, cols] = lax.dot_general(
                hid[o, :], dw[cols, :], (((1,), (1,)), ((), ())), preferred_element_type=F32
            ).astype(BF)

        tiles(body)
        for cp in c1(q, r):
            cp.start()

    def c2(q, r):
        n = q * 2 + r
        return remote(
            part.at[side(q, r, 4, send_of(q, r, True))],
            c2buf.at[chunk(q, r)],
            c2_send.at[n], c2_recv.at[n], at(z, mate, c),
        )

    def add_rows(target, buffers, count):
        def step(i, carry):
            total = part[pl.ds(pl.multiple_of(target.start + i * 16, 16), 16), :].astype(F32)
            for buf, other in buffers:
                total += buf[pl.ds(pl.multiple_of(other.start + i * 16, 16), 16), :].astype(F32)
            part[pl.ds(pl.multiple_of(target.start + i * 16, 16), 16), :] = total.astype(BF)
            return carry

        lax.fori_loop(0, count // 16, step, 0)

    def c2_start(q, r):
        c1(q, r)[0].wait_recv()
        add_rows(side(q, r, 4, send_of(q, r, True)), [(c1buf, side(q, r, 2, 1))], LEN[r])
        c2(q, r).start()

    def c3(q, r):
        src = part.at[side(q, r, 4, keep_of(q, r, True))]
        dst = home.at[chunk(0, r)]
        if q:
            dst = zout.at[chunk(q - 1, r)]
        u = even(q, r)
        n = q * 2 + r
        return (
            remote(src, dst, c3_send.at[n], zo_recv.at[n], at(z, u * x + (1 - u) * near, pair)),
            pltpu.make_async_copy(src, dst, zo_recv.at[n]),
            u * serve,
        )

    def c3_start(q, r):
        c1(q, r)[1].wait_recv()
        c2(q, r).wait_recv()
        add_rows(
            side(q, r, 4, keep_of(q, r, True)),
            [(c1buf, side(q, r, 2, 0)), (c2buf, chunk(q, r))],
            LEN[r],
        )
        away, local, here = c3(q, r)

        @pl.when(here == 1)
        def _():
            local.start()

        @pl.when(here == 0)
        def _():
            away.start()

    def back(q, r):
        n = (q - 1) * 2 + r
        return remote(
            zout.at[chunk(q - 1, r)], home.at[chunk(q, r)],
            b_send.at[n], b_recv.at[n], at((z + 4 - q) % 4, x, c),
        )

    def back_start(q, r):
        arrived(zout.at[chunk(q - 1, r)], zo_recv.at[q * 2 + r])
        back(q, r).start()

    def swap(k):
        return remote(
            ex_send.at[:, piece(k)], ex_recv.at[:, piece(k)], e_send.at[k], e_recv.at[k], sibling
        )

    def mix(q, parts, start=False, last=False):
        for r in parts:
            if q:
                back(q, r).wait_recv()
            else:
                arrived(home.at[chunk(0, r)], zo_recv.at[r])
        s = chunk(q, 0) if len(parts) == 1 else pl.ds(q * CH, CH)
        if parts == (1,):
            s = chunk(q, 1)

        def body(cols):
            value = lax.dot_general(
                weight_t[s, :], home[s, cols], (((0,), (0,)), ((), ())),
                preferred_element_type=F32,
            )
            if not start:
                value += acc[:, cols]
            if last:
                acc[pl.ds(0, 128), cols] = value[:128]
                ex_send[:, cols] = value[128:].astype(BF)
            else:
                acc[:, cols] = value

        for k in range(K):
            tiles(body, k * WIDE, WIDE)
            if last:
                swap(k).start()

    def join(k):
        swap(k).wait()

        def body(cols):
            mixed_ref[:, cols] = (
                acc[pl.ds(0, 128), cols] + ex_recv[:, cols].astype(F32)
            ).astype(BF)

        tiles(body, k * WIDE, WIDE)

    def pick():
        for j in range(3):
            loads[4 + j].wait()
        for cp in y_copies:
            cp.wait_send()
        for d in (1, 2, 3):
            for j in range(3):
                arrived(cand.at[((4 - d) % 4) * 3 + j], y_recv.at[(d - 1) * 3 + j])
        asked = donor_ref[y * 2 + 1 - zl, ep]
        asked_y = (asked // 2 + 4 - y) % 4
        for j in range(3):
            lsend[j] = cand[asked_y * 3 + j]

    l_copy = remote(lsend, lrecv, l_send, l_recv, partner)

    def land():
        l_copy.wait()
        wanted = donor_ref[grp, ep]
        wanted_y = (wanted // 2 + 4 - y) % 4
        wanted_z = wanted % 2
        from_here = jnp.full((SPAN, F), wanted_z, jnp.int32) == zl
        for j in range(3):
            close = cand[wanted_y * 3 + j].astype(F32)
            far = lrecv[j].astype(F32)
            landed_ref[j] = jnp.where(from_here, close, far).astype(BF)

    sib_tok(0).wait_recv()
    pack_chunk(2, 0)
    pack_chunk(0, 0)
    sib_tok(1).wait_recv()
    pack_chunk(2, 1)
    z_copy(2, 0).start()
    z_copy(2, 1).start()
    pack_chunk(0, 1)
    fan_start(0, 0)
    fan_start(0, 1)
    pack_chunk(1, 0)
    pack_chunk(1, 1)
    z_copy(1, 0).start()
    pack_chunk(3, 0)
    pack_chunk(3, 1)
    z_copy(3, 0).start()
    z_copy(1, 1).start()
    z_copy(3, 1).start()
    relay_near(0, 0)
    for n in (1, 2, 3):
        loads[n].wait()
    relay_rest(0, 0)
    relay_near(0, 1)
    up(0, 0)
    down(0, 0)
    relay_rest(0, 1)
    c2_start(0, 0)
    up(0, 1)
    down(0, 1)
    z_copy(2, 0).wait_recv()
    fan_start(2, 0)
    c2_start(0, 1)
    relay_near(2, 0)
    relay_rest(2, 0)
    c3_start(0, 0)
    z_copy(2, 1).wait_recv()
    fan_start(2, 1)
    up(2, 0)
    down(2, 0)
    c3_start(0, 1)
    c2_start(2, 0)
    relay_near(2, 1)
    relay_rest(2, 1)
    pick()
    up(2, 1)
    down(2, 1)
    mix(0, (0, 1), start=True)
    c2_start(2, 1)
    z_copy(1, 0).wait_recv()
    fan_start(1, 0)
    z_copy(3, 0).wait_recv()
    fan_start(3, 0)
    c3_start(2, 0)
    back_start(2, 0)
    relay_near(1, 0)
    relay_near(3, 0)
    relay_rest(1, 0)
    relay_rest(3, 0)
    c3_start(2, 1)
    back_start(2, 1)
    z_copy(1, 1).wait_recv()
    fan_start(1, 1)
    z_copy(3, 1).wait_recv()
    fan_start(3, 1)
    l_copy.start()
    up(1, 0)
    down(1, 0)
    up(3, 0)
    down(3, 0)
    relay_near(1, 1)
    relay_near(3, 1)
    c2_start(1, 0)
    c2_start(3, 0)
    relay_rest(1, 1)
    relay_rest(3, 1)
    up(1, 1)
    down(1, 1)
    up(3, 1)
    down(3, 1)
    c2_start(1, 1)
    c2_start(3, 1)
    c3_start(1, 0)
    back_start(1, 0)
    c3_start(3, 0)
    back_start(3, 0)
    land()
    mix(2, (0, 1))
    c3_start(1, 1)
    back_start(1, 1)
    c3_start(3, 1)
    back_start(3, 1)
    mix(1, (0,))
    mix(3, (0,))
    mix(1, (1,))
    mix(3, (1,), last=True)
    join(0)
    join(1)
    sib_meta.wait_send()
    for k in range(K):
        sib_tok(k).wait_send()
    for q in range(4):
        for r in range(2):
            away, over, _, beyond = fan(q, r)
            away.wait_send()

            @pl.when(serve == 1)
            def _():
                over.wait_send()

            @pl.when(serve == 0)
            def _():
                beyond.wait_send()

            @pl.when(even(q, r) == 1)
            def _():
                relay(q, r, cross).wait_send()

            @pl.when(even(q, r) == 0)
            def _():
                relay(q, r, near).wait_send()
                relay(q, r, mate).wait_send()

            for cp in c1(q, r):
                cp.wait_send()
            c2(q, r).wait_send()
            away, _, here = c3(q, r)

            @pl.when(here == 0)
            def _():
                away.wait_send()

            if q:
                z_copy(q, r).wait_send()
                back(q, r).wait_send()


def on_device(tokens, expert_ids, gate_weights, donor_group, gate_pieces, up_pieces, down_pieces):
    tok = tokens.reshape(128, D)
    ids = expert_ids.reshape(128, 2).T.astype(F32)
    wts = gate_weights.reshape(128, 2).T
    meta = jnp.concatenate([ids, wts, jnp.zeros((4, 128), F32)], axis=0)
    vmem, hbm = pltpu.VMEM, pl.ANY
    dma = pltpu.SemaphoreType.DMA
    mixed, landed = pl.pallas_call(
        layer,
        out_shape=(
            jax.ShapeDtypeStruct((128, D), BF),
            jax.ShapeDtypeStruct((3, SPAN, F), BF),
        ),
        in_specs=[
            pl.BlockSpec(memory_space=hbm),
            pl.BlockSpec(memory_space=vmem),
            pl.BlockSpec(memory_space=pltpu.SMEM),
            pl.BlockSpec(memory_space=hbm),
            pl.BlockSpec(memory_space=hbm),
            pl.BlockSpec(memory_space=hbm),
        ],
        out_specs=(pl.BlockSpec(memory_space=vmem), pl.BlockSpec(memory_space=vmem)),
        scratch_shapes=[
            vmem((256, D), BF),
            vmem((8, 128), F32),
            vmem((4 * CH, 256), BF),
            vmem((4 * CH, 256), BF),
            vmem((4 * CH, D), BF),
            vmem((3 * CH, D), BF),
            vmem((16 * CH, D), BF),
            vmem((D, F), BF),
            vmem((D, F), BF),
            vmem((D, F), BF),
            vmem((4 * CH, F), F32),
            vmem((4 * CH, F), F32),
            vmem((16 * CH, F), BF),
            vmem((16 * CH, D), BF),
            vmem((8 * CH, D), BF),
            vmem((4 * CH, D), BF),
            vmem((3 * CH, D), BF),
            vmem((4 * CH, D), BF),
            vmem((256, D), F32),
            vmem((128, D), BF),
            vmem((128, D), BF),
            vmem((12, SPAN, F), BF),
            vmem((3, SPAN, F), BF),
            vmem((3, SPAN, F), BF),
            dma((7,)),
            dma, dma,
            dma((K,)), dma((K,)),
            dma((6,)), dma((6,)),
            dma((16,)), dma((32,)), dma((32,)),
            dma((16,)), dma((16,)),
            dma((8,)), dma((8,)),
            dma((8,)), dma((8,)),
            dma((6,)), dma((6,)),
            dma((9,)), dma((9,)),
            dma, dma,
            dma((K,)), dma((K,)),
        ],
        compiler_params=pltpu.CompilerParams(
            collective_id=0, has_side_effects=True, vmem_limit_bytes=62 * 2**20
        ),
        cost_estimate=pl.CostEstimate(
            flops=8 * 10**9, bytes_accessed=10**7, transcendentals=4 * 10**5
        ),
    )(tok, meta, donor_group, gate_pieces[0], up_pieces[0], down_pieces[0])
    return mixed.reshape(2, 64, D), landed


def solution(mesh):
    in_specs = (
        P(None, ("grp", "ep"), None),
        P(None, ("grp", "ep"), None),
        P(None, ("grp", "ep"), None),
        P(),
        P(("grp", "ep"), None, None),
        P(("grp", "ep"), None, None),
        P(("grp", "ep"), None, None),
    )
    out_specs = (P(None, ("grp", "ep"), None), P(None, ("grp", "ep"), None))
    return jax.shard_map(
        on_device, mesh=mesh, in_specs=in_specs, out_specs=out_specs, check_vma=False
    )
```

time: 189 us -> 162 us (0.86)
  the two profiles are of different devices: /device:TPU:91 before, /device:TPU:33 now
where the time goes in v2:
time: 162 us
  Pallas kernels  156 us (96%)
  local copies, waits for them, and re-layouts  4.01 us (2%)
    pallas_call x1, Pallas kernels, on_device(): pl.pallas_call(layer, out_shape=(jax.ShapeDtypeStruct((128, D), BF), jax....  156 us
    unnamed x5, local copies, waits for them, and re-layouts  3.76 us

profile of v2, /device:TPU:33, one launch (start us, length us, event | category | flops | bytes accessed | tf_op | source)
XLA Modules:
  0.0 162.0 jit_solution(2888362904564796198)
XLA Ops:
  0.6 0.1 pad.2.clone
  0.7 0.7 convert_element_type.9
  1.4 0.1 convert_element_type.10
  1.5 0.7 copy.10
  2.2 0.1 reshape.16
  2.3 0.7 maximum_maximum_fusion.meta_ref
  2.9 156.0 %shard_map.86 = (bf16[128,3584]{1,0:T(8,128)(2,1)}, bf16[3,448,256]{2,1,0:T(8,128)(2,1)}) custom-call(bf16[128,3584]{1,0:T(8,128)(2,1)} %bitcast.17, f32[8,128]{1,0:T(8,128)} %maximum_maximum_fusion.meta_ref, s32[8,32]{1,0:T(8,128)} %donor_ref.1, bf16[3584,256]{1,0:T(8,128)(2,1)} %bitcast.14, bf16[3584,256]{1,0:T(8,128)(2,1)} %bitcast.15, ...), custom_call_target="tpu_custom_call" | custom-call | flops 8000000000 | bytes 10000000 | tf_op jit(solution)/shard_map/pallas_call | solution.py:561
  158.9 0.0 copy-start
  158.9 2.2 %copy.13 = bf16[2,64,3584]{2,1,0:T(8,128)(2,1)} copy(bf16[2,64,3584]{2,1,0:T(8,128)(2,1)} %bitcast.11) | data formatting | bytes 1835008
  161.1 0.0 copy-done
  161.1 0.8 copy.14
  (2 shorter events, 0.0 us)
Async XLA Ops:
  158.9 2.2 %copy-start = (bf16[3,448,256]{2,1,0:T(8,128)(2,1)S(1)}, bf16[3,448,256]{2,1,0:T(8,128)(2,1)}, u32[]{:S(2)}) copy-start(bf16[3,448,256]{2,1,0:T(8,128)(2,1)} %get-tuple-element.9) | copy-start | bytes 2064388

commit v3 on v2

--- a/solution.py
+++ b/solution.py
@@ -14,8 +14,8 @@
 K = 2
 WIDE = D // K
 TILE = 896
-LEN = (48, 32)
-OFF = (0, 48)
+LEN = (32, 48)
+OFF = (0, 32)
 SPAN = 448
 BF = jnp.bfloat16
 F32 = jnp.float32
@@ -416,100 +416,102 @@
             landed_ref[j] = jnp.where(from_here, close, far).astype(BF)
 
     sib_tok(0).wait_recv()
-    pack_chunk(2, 0)
+    pack_chunk(1, 0)
+    pack_chunk(3, 0)
+    sib_tok(1).wait_recv()
+    pack_chunk(1, 1)
+    z_copy(1, 0).start()
+    pack_chunk(3, 1)
+    z_copy(3, 0).start()
     pack_chunk(0, 0)
-    sib_tok(1).wait_recv()
-    pack_chunk(2, 1)
-    z_copy(2, 0).start()
-    z_copy(2, 1).start()
     pack_chunk(0, 1)
     fan_start(0, 0)
     fan_start(0, 1)
-    pack_chunk(1, 0)
-    pack_chunk(1, 1)
-    z_copy(1, 0).start()
-    pack_chunk(3, 0)
-    pack_chunk(3, 1)
-    z_copy(3, 0).start()
+    pack_chunk(2, 0)
+    pack_chunk(2, 1)
+    z_copy(2, 0).start()
     z_copy(1, 1).start()
     z_copy(3, 1).start()
+    z_copy(2, 1).start()
     relay_near(0, 0)
     for n in (1, 2, 3):
         loads[n].wait()
     relay_rest(0, 0)
-    relay_near(0, 1)
     up(0, 0)
     down(0, 0)
+    relay_near(0, 1)
     relay_rest(0, 1)
-    c2_start(0, 0)
-    up(0, 1)
-    down(0, 1)
-    z_copy(2, 0).wait_recv()
-    fan_start(2, 0)
-    c2_start(0, 1)
-    relay_near(2, 0)
-    relay_rest(2, 0)
-    c3_start(0, 0)
-    z_copy(2, 1).wait_recv()
-    fan_start(2, 1)
-    up(2, 0)
-    down(2, 0)
-    c3_start(0, 1)
-    c2_start(2, 0)
-    relay_near(2, 1)
-    relay_rest(2, 1)
-    pick()
-    up(2, 1)
-    down(2, 1)
-    mix(0, (0, 1), start=True)
-    c2_start(2, 1)
     z_copy(1, 0).wait_recv()
     fan_start(1, 0)
     z_copy(3, 0).wait_recv()
     fan_start(3, 0)
-    c3_start(2, 0)
-    back_start(2, 0)
+    up(0, 1)
+    down(0, 1)
     relay_near(1, 0)
     relay_near(3, 0)
+    z_copy(2, 0).wait_recv()
+    fan_start(2, 0)
     relay_rest(1, 0)
     relay_rest(3, 0)
-    c3_start(2, 1)
-    back_start(2, 1)
+    up(1, 0)
+    down(1, 0)
+    c2_start(1, 0)
+    up(3, 0)
+    down(3, 0)
+    c2_start(3, 0)
     z_copy(1, 1).wait_recv()
     fan_start(1, 1)
     z_copy(3, 1).wait_recv()
     fan_start(3, 1)
+    relay_near(2, 0)
+    relay_rest(2, 0)
+    up(2, 0)
+    down(2, 0)
+    c2_start(2, 0)
+    pick()
+    z_copy(2, 1).wait_recv()
+    fan_start(2, 1)
     l_copy.start()
-    up(1, 0)
-    down(1, 0)
-    up(3, 0)
-    down(3, 0)
+    c3_start(1, 0)
+    c3_start(3, 0)
     relay_near(1, 1)
     relay_near(3, 1)
-    c2_start(1, 0)
-    c2_start(3, 0)
+    back_start(1, 0)
+    back_start(3, 0)
     relay_rest(1, 1)
     relay_rest(3, 1)
     up(1, 1)
     down(1, 1)
+    c2_start(1, 1)
     up(3, 1)
     down(3, 1)
-    c2_start(1, 1)
     c2_start(3, 1)
-    c3_start(1, 0)
-    back_start(1, 0)
-    c3_start(3, 0)
-    back_start(3, 0)
+    c3_start(2, 0)
+    relay_near(2, 1)
+    relay_rest(2, 1)
+    back_start(2, 0)
+    up(2, 1)
+    down(2, 1)
+    c2_start(2, 1)
+    c2_start(0, 0)
+    c2_start(0, 1)
+    c3_start(1, 1)
+    c3_start(3, 1)
+    back_start(1, 1)
+    back_start(3, 1)
+    mix(1, (0,), start=True)
+    c3_start(2, 1)
+    mix(3, (0,))
+    back_start(2, 1)
+    mix(2, (0,))
+    c3_start(0, 0)
+    c3_start(0, 1)
     land()
-    mix(2, (0, 1))
-    c3_start(1, 1)
-    back_start(1, 1)
-    c3_start(3, 1)
-    back_start(3, 1)
-    mix(1, (0,))
-    mix(3, (0,))
     mix(1, (1,))
-    mix(3, (1,), last=True)
+    mix(3, (1,))
+    mix(2, (1,))
+    mix(0, (0,))
+    mix(0, (1,), last=True)
     join(0)
     join(1)
     sib_meta.wait_send()

time: 162 us -> 151 us (0.932)
  the two profiles are of different devices: /device:TPU:33 before, /device:TPU:91 now
where the time goes in v3:
time: 151 us
  Pallas kernels  145 us (96%)
  local copies, waits for them, and re-layouts  4.01 us (3%)
    pallas_call x1, Pallas kernels, on_device(): pl.pallas_call(layer, out_shape=(jax.ShapeDtypeStruct((128, D), BF), jax....  145 us
    unnamed x5, local copies, waits for them, and re-layouts  3.76 us

profile of v3, /device:TPU:91, one launch (start us, length us, event | category | flops | bytes accessed | tf_op | source)
XLA Modules:
  0.0 150.7 jit_solution(8900026277534697014)
XLA Ops:
  0.6 0.1 pad.2.clone
  0.7 0.7 convert_element_type.9
  1.4 0.1 convert_element_type.10
  1.5 0.7 copy.10
  2.2 0.1 reshape.16
  2.3 0.7 maximum_maximum_fusion.meta_ref
  2.9 144.7 %shard_map.86 = (bf16[128,3584]{1,0:T(8,128)(2,1)}, bf16[3,448,256]{2,1,0:T(8,128)(2,1)}) custom-call(bf16[128,3584]{1,0:T(8,128)(2,1)} %bitcast.17, f32[8,128]{1,0:T(8,128)} %maximum_maximum_fusion.meta_ref, s32[8,32]{1,0:T(8,128)} %donor_ref.1, bf16[3584,256]{1,0:T(8,128)(2,1)} %bitcast.14, bf16[3584,256]{1,0:T(8,128)(2,1)} %bitcast.15, ...), custom_call_target="tpu_custom_call" | custom-call | flops 8000000000 | bytes 10000000 | tf_op jit(solution)/shard_map/pallas_call | solution.py:563
  147.6 0.0 copy-start
  147.6 2.2 %copy.13 = bf16[2,64,3584]{2,1,0:T(8,128)(2,1)} copy(bf16[2,64,3584]{2,1,0:T(8,128)(2,1)} %bitcast.11) | data formatting | bytes 1835008
  149.9 0.0 copy-done
  149.9 0.8 copy.14
  (2 shorter events, 0.0 us)
Async XLA Ops:
  147.6 2.2 %copy-start = (bf16[3,448,256]{2,1,0:T(8,128)(2,1)S(1)}, bf16[3,448,256]{2,1,0:T(8,128)(2,1)}, u32[]{:S(2)}) copy-start(bf16[3,448,256]{2,1,0:T(8,128)(2,1)} %get-tuple-element.9) | copy-start | bytes 2064388

commit v4 on v3

--- a/solution.py
+++ b/solution.py
@@ -169,7 +169,7 @@
         if q:
             src = zin.at[chunk(q - 1, r)]
         dst = xin.at[side(q, r, 4, x)]
-        f = (q // 2 + x + r) % 2
+        f = (q + x + r) % 2
         n = q * 2 + r
         recv = x_recv.at[n * 4 + x]
         t0 = at(z, serve * mate + (1 - serve) * near, f)
@@ -194,7 +194,7 @@
             beyond.start()
 
     def even(q, r):
-        return 1 - (x + c + q // 2 + r) % 2
+        return 1 - (x + c + q + r) % 2
 
     def x_wait(q, r, xs):
         arrived(xin.at[side(q, r, 4, xs)], x_recv.at[(q * 2 + r) * 4 + xs])

time: 151 us -> 150 us (level)
  no operation moved by 1% of the time
where the time goes in v4:
time: 150 us
  Pallas kernels  144 us (96%)
  local copies, waits for them, and re-layouts  4.01 us (3%)
    pallas_call x1, Pallas kernels, on_device(): pl.pallas_call(layer, out_shape=(jax.ShapeDtypeStruct((128, D), BF), jax....  144 us
    unnamed x5, local copies, waits for them, and re-layouts  3.76 us

profile of v4, /device:TPU:91, one launch (start us, length us, event | category | flops | bytes accessed | tf_op | source)
XLA Modules:
  0.0 150.0 jit_solution(7706325776416339664)
XLA Ops:
  0.6 0.1 pad.2.clone
  0.7 0.7 convert_element_type.9
  1.4 0.1 convert_element_type.10
  1.5 0.7 copy.10
  2.2 0.1 reshape.16
  2.3 0.7 maximum_maximum_fusion.meta_ref
  2.9 144.0 %shard_map.86 = (bf16[128,3584]{1,0:T(8,128)(2,1)}, bf16[3,448,256]{2,1,0:T(8,128)(2,1)}) custom-call(bf16[128,3584]{1,0:T(8,128)(2,1)} %bitcast.17, f32[8,128]{1,0:T(8,128)} %maximum_maximum_fusion.meta_ref, s32[8,32]{1,0:T(8,128)} %donor_ref.1, bf16[3584,256]{1,0:T(8,128)(2,1)} %bitcast.14, bf16[3584,256]{1,0:T(8,128)(2,1)} %bitcast.15, ...), custom_call_target="tpu_custom_call" | custom-call | flops 8000000000 | bytes 10000000 | tf_op jit(solution)/shard_map/pallas_call | solution.py:563
  146.9 0.0 copy-start
  146.9 2.2 %copy.13 = bf16[2,64,3584]{2,1,0:T(8,128)(2,1)} copy(bf16[2,64,3584]{2,1,0:T(8,128)(2,1)} %bitcast.11) | data formatting | bytes 1835008
  149.2 0.0 copy-done
  149.2 0.8 copy.14
  (2 shorter events, 0.0 us)
Async XLA Ops:
  146.9 2.2 %copy-start = (bf16[3,448,256]{2,1,0:T(8,128)(2,1)S(1)}, bf16[3,448,256]{2,1,0:T(8,128)(2,1)}, u32[]{:S(2)}) copy-start(bf16[3,448,256]{2,1,0:T(8,128)(2,1)} %get-tuple-element.9) | copy-start | bytes 2064388
